TPU v7x, 512 devices: a whole 4x8x8 slice. The times are simulated.
512 devices in a mesh: bx: 8 (over z), by: 16 (over y, core), freq: 4 (over x).
Axes of the slice: x: 4, y: 8, z: 8, core: 2. Of those that a mesh axis runs over, the one named last changes fastest.
Arguments:
- leaf_maps: float32 [32, 16, 256, 256], P(('freq', 'bx'), 'by'), parts along dimension 0, as said below
- leaf_operator: float32 [472, 472], replicated, as said below
- region_eps: float32 [8, 472], replicated, may hold values from 1 to 12
- wave_sq: float32 [4], P('freq'), parts along dimension 0, may hold values from 0.01 to 0.06
- region_labels: int32 [8, 16], P('bx', 'by'), may hold values from 0 to 7
- build_flags: int32 [8, 16], P('bx', 'by'), may hold values from 0 to 1, as said below
Outputs:
- dtn_rows: float32 [32, 16, 96, 768], P(('freq', 'bx'), 'by'), parts along dimension 0
There are 4 independent parts, one for each index of `freq`. A program takes and returns all parts, laid end to end along the dimension named above; an argument that names none is the same for every part. Nothing has to cross between parts.
Inputs may be any that keep to these rules, and one draw needn't show every extreme that they name: Every leaf_maps[i, j] is symmetric up to rounding with all eigenvalues 1 or more. leaf_operator is symmetric up to rounding, and leaf_operator minus any diagonal matrix with entries below 1 is positive definite. `build_flags`: exactly max(1, 16) leaves are flagged.
All inputs are finite; a program needn't handle non-finite values.
Results may differ from a plain program's by a relative error of at most 0.0003.
Values sent between devices are 32-bit elements; how exact they have to be, the bound alone decides.
No kernel may reach another device: no remote copies, remote signals or barrier semaphores. Data moves between devices by JAX's collectives and lax.ppermute only.
A program may use at most 64 MiB of HBM per device.

v0:
```python
import jax
import jax.numpy as jnp
from jax import lax
from jax.experimental import pallas as pl
from jax.experimental.pallas import tpu as pltpu
from jax.sharding import PartitionSpec as P

FACE = 64
LEAF = 4 * FACE
CUT_TWO, CUT_THREE = 200, 160
F32 = jnp.float32
BF16 = jnp.bfloat16


LONG = pl.CostEstimate(flops=10**10, bytes_accessed=10**8, transcendentals=10**6)


def swapped(shard, axis, stride):
    return lax.ppermute(shard, axis, [(i, i ^ 1 << stride) for i in range(lax.axis_size(axis))])


def split(x):
    high = x.astype(BF16)
    return high, (x - high.astype(F32)).astype(BF16)


def thirds(x):
    high = x.astype(BF16).astype(F32)
    rest = x - high
    middle = rest.astype(BF16).astype(F32)
    return high, middle, (rest - middle).astype(BF16).astype(F32)


def dot(a, b):
    return jnp.dot(a, b, preferred_element_type=F32)


def product(a, b):
    (a_high, a_low), (b_high, b_low) = a, b
    depth = a_high.shape[1]
    if depth % 128 and depth != FACE:
        return dot(a_high, b_high) + (dot(a_high, b_low) + dot(a_low, b_high))
    twice = dot(
        jnp.concatenate([a_high, a_low], axis=1), jnp.concatenate([b_high, b_high], axis=0)
    )
    return twice + dot(a_high, b_low)


def tree(terms):
    while len(terms) > 1:
        terms = [x + y for x, y in zip(terms[::2], terms[1::2])]
    return terms[0]


def minus(value, terms):
    for term in terms:
        value = value - term
    return value


def spd_inverse(matrix, left=None, both=False, panel=4, look=4, half=4):
    size = matrix.shape[0]
    shape = (8, size)
    count = size // 8
    tiles = [matrix[8 * g : 8 * g + 8] for g in range(count)]
    lane = lax.broadcasted_iota(jnp.int32, shape, 1)
    sub = lax.broadcasted_iota(jnp.int32, shape, 0)

    def column(tile, c):
        return jnp.broadcast_to(tile[:, c : c + 1], shape)

    def row(tile, r):
        return jnp.broadcast_to(tile[r : r + 1, :], shape)

    def inside(start, stop):
        return (lane >= start) & (lane < stop)

    pivot = [column(tiles[0], j) for j in range(8)]
    head = row(pivot[0], 0)
    for start in range(0, count, panel):
        stop = min(start + panel, count)
        last = min(stop + look, count)
        outside = [*range(last, count), *range(start if left is None or both else 0)]
        if outside:
            strip = jnp.concatenate([tiles[g] for g in outside], axis=0)[:, 8 * start : 8 * stop]
            high, middle, low = thirds(strip)
            factors = jnp.concatenate([high, high, middle, high, low, middle], axis=1).astype(BF16)
        for k in range(start, stop):
            first = 8 * k
            block = inside(first, first + 8)
            rows = jnp.where(block, (lane - first == sub).astype(F32), tiles[k])
            ahead = k + 1 < count
            if ahead:
                after = jnp.where(block, 0.0, tiles[k + 1])
                side = [column(tiles[k + 1], first + j) for j in range(8)]
            scale = None
            for p in range(8):
                inverse = pl.reciprocal(head, approx=True)
                if p < 7:
                    element = row(pivot[p + 1], p)
                    head = row(pivot[p + 1], p + 1) - element * (element * inverse)
                factor = jnp.where(sub == p, 0.0, pivot[p]) * inverse
                picked = row(rows, p)
                if ahead:
                    edge = side[p]
                    factor_ahead = edge * inverse
                    if p == half:
                        coming = [column(after, first + 8 + j) for j in range(8)]
                    if p == 7:
                        element = row(edge, 0)
                        head = row(coming[0], 0) - element * (element * inverse)
                    if p >= half:
                        for j in range(8):
                            coming[j] = coming[j] - factor_ahead * row(edge, j)
                    after = after - factor_ahead * picked
                for j in range(p + 1, 8):
                    element = row(pivot[j], p)
                    pivot[j] = pivot[j] - factor * element
                    if ahead:
                        side[j] = side[j] - factor_ahead * element
                rows = rows - factor * picked
                scale = inverse if scale is None else jnp.where(sub == p, inverse, scale)
            rows = rows * scale
            picked = [row(rows, j) for j in range(8)]
            for g in range(start, last):
                if g == k:
                    tiles[g] = rows
                elif g == k + 1:
                    tiles[g] = after
                else:
                    terms = [column(tiles[g], first + j) * picked[j] for j in range(8)]
                    cleared = jnp.where(block, 0.0, tiles[g])
                    tiles[g] = cleared - tree(terms) if count <= panel else minus(cleared, terms)
            if ahead:
                pivot = coming
        solved = jnp.concatenate(tiles[start:stop], axis=0)
        if outside:
            high, middle, low = thirds(solved)
            right = jnp.concatenate([high, middle, high, low, high, middle], axis=0).astype(BF16)
            update = dot(factors, right)
            block = inside(8 * start, 8 * stop)
            for i, g in enumerate(outside):
                tiles[g] = jnp.where(block, 0.0, tiles[g]) - update[8 * i : 8 * i + 8]
        if left is not None:
            blanks = [jnp.zeros((rows, size), BF16) for rows in (8 * start, size - 8 * stop)]
            right = [
                jnp.concatenate([x for x in (blanks[0], part, blanks[1]) if x.shape[0]], axis=0)
                for part in split(solved)
            ]
            columns = lax.broadcasted_iota(jnp.int32, left.shape, 1)
            block = (columns >= 8 * start) & (columns < 8 * stop)
            left = jnp.where(block, 0.0, left) - product(split(left), right)
    if left is not None and not both:
        return left
    whole = jnp.concatenate(tiles, axis=0)
    return (whole, left) if both else whole


def build_kernel(label, flag, wave, given, operator, table_at, out, table, one, two, edge, sems):
    size = operator.shape[0]
    middle = LEAF + 128
    copies = [
        pltpu.make_async_copy(source, target, sems.at[i])
        for i, (source, target) in enumerate(
            (
                (operator.at[pl.ds(LEAF, 128)], one),
                (table_at, table),
                (operator.at[pl.ds(middle, size - middle)], two),
                (operator.at[pl.ds(0, LEAF)], edge),
                (given, out),
            )
        )
    ]
    flagged = flag[0, 0] > 0

    @pl.when(jnp.logical_not(flagged))
    def _():
        copies[4].start()
        copies[4].wait()

    @pl.when(flagged)
    def _():
        for copy in copies[:4]:
            copy.start()
        for copy in copies[:2]:
            copy.wait()
        shift = wave[0] * table[pl.ds(label[0, 0], 1), :]
        border, near, far = slice(0, LEAF), slice(LEAF, middle), slice(middle, size)

        def shifted(ref, span):
            block = ref[:, span]
            ids = lax.broadcasted_iota(jnp.int32, block.shape, 0)
            diagonal = ids == lax.broadcasted_iota(jnp.int32, block.shape, 1)
            return block - jnp.where(diagonal, shift[:, span], 0.0)

        right = split(one[:, border]), split(one[:, far])
        copies[2].wait()
        inverse, left = spd_inverse(shifted(one, near), two[:, near], both=True)
        copies[3].wait()
        left = split(left)
        inner = shifted(two, far) + product(left, right[1])
        coupled = split(two[:, border] + product(left, right[0]))
        left = split(edge[:, near])
        left = split(product(left, split(inverse)))
        merged = shifted(edge, border) - product(left, right[0])
        across = split(edge[:, far] - product(left, right[1]))
        inverse = split(spd_inverse(inner))
        solved = split(product(inverse, coupled))
        out[...] = merged - product(across, solved)


def halves(shape):
    return lax.broadcasted_iota(jnp.int32, shape, 1) < FACE


def turn(tile):
    return pltpu.roll(tile, FACE, 1)


def leaf_rows(place, mine, theirs):
    across, third, lead = place[0], place[1], place[2]
    is_alpha = lead == 0
    left = halves((FACE, 128))

    def load(alpha, block, tile):
        spot = pl.ds(pl.multiple_of(block * FACE, FACE), FACE)
        span = slice(128 * tile, 128 * tile + 128)
        own = is_alpha if alpha else jnp.logical_not(is_alpha)
        return jnp.where(own, mine[spot, span], theirs[spot, span])

    def alpha_rows(block):
        sides = load(True, block, 0)
        ends = load(True, block, 1)
        sides = jnp.where(across == 0, turn(sides), sides)
        tiles = (
            jnp.where(left, sides, 0.0),
            jnp.where(left, jnp.where(third == 0, 0.0, ends), sides),
            jnp.where(left & (third == 0), ends, 0.0),
        )
        return jnp.concatenate(tiles, axis=1), turn(ends)

    def beta_rows(block):
        sides = load(False, block, 0)
        ends = load(False, block, 1)
        other = turn(sides)
        near_far = jnp.where(across == 0, other, sides)
        far_near = jnp.where(across == 0, sides, other)
        flipped = turn(ends)
        tiles = (
            jnp.where(left, 0.0, far_near),
            jnp.where(left & (third == 0), flipped, 0.0),
            jnp.where(
                third == 0,
                jnp.where(left, 0.0, near_far),
                jnp.where(left, far_near, ends),
            ),
        )
        return jnp.concatenate(tiles, axis=1), ends

    return alpha_rows, beta_rows


def either(flag, one, other):
    return [jnp.where(flag, x, y) for x, y in zip(one, other)]


def stacked(one, two, start, stop):
    cut = one.shape[0]
    parts = []
    if start < cut:
        parts.append(one[start : min(stop, cut), :])
    if stop > cut:
        parts.append(two[max(start, cut) - cut : stop - cut, :])
    return jnp.concatenate(parts, axis=0)


def stack(one, two, start, value):
    cut = one.shape[0]
    stop = start + value.shape[0]
    if start < cut:
        one[start : min(stop, cut), :] = value[: cut - start]
    if stop > cut:
        two[max(start, cut) - cut : stop - cut, :] = value[max(cut - start, 0) :]


def first_kernel(place, mine, theirs, message_one, message_two, link, solved_high, solved_low):
    alpha_rows, beta_rows = leaf_rows(place, mine, theirs)
    near = jnp.where(place[0] == 0, 1, 0)
    tiles_a, meet_a = alpha_rows(3)
    tiles_b, meet_b = beta_rows(2)
    system = (meet_a + meet_b)[:, :FACE]
    right = split(tiles_a + tiles_b)
    parts = [alpha_rows(near), beta_rows(near), either(place[1] == 0, beta_rows(3), alpha_rows(2))]
    direct = jnp.concatenate([tiles for tiles, _ in parts], axis=0)
    coupling = split(jnp.concatenate([meet for _, meet in parts], axis=0)[:, :FACE])
    inverse = split(spd_inverse(system, panel=8))
    solved = split(product(inverse, right))
    merged = direct - product(coupling, solved)
    for i in range(3):
        stack(message_one, message_two, 128 * i, merged[0:128, 128 * i : 128 * i + 128])
    stack(message_one, message_two, 384, merged[128:192, 128:256])
    stack(message_one, message_two, 448, merged[128:192, 256:384])
    link[...] = merged[128:192, 0:128]
    solved_high[...], solved_low[...] = solved


def rows_kernel(place, mine, theirs, solved_high, solved_low, outer, direct, coupling):
    alpha_rows, beta_rows = leaf_rows(place, mine, theirs)
    third, lead = place[1], place[2]
    far = jnp.where(place[0] == 0, 0, 1)
    direct[0:64, :], coupling[0:64, :] = alpha_rows(far)
    at_two = alpha_rows(2)
    at_far = beta_rows(far)
    at_three = beta_rows(3)
    direct[64:128, :], coupling[64:128, :] = either(third == 0, at_two, at_far)
    direct[128:192, :], coupling[128:192, :] = either(third == 0, at_far, at_three)
    spot = pl.ds(pl.multiple_of(lead * 96, 32), 96)
    solved = solved_high[...], solved_low[...]
    outer[...] = direct[spot, :] - product(split(coupling[spot, :][:, :FACE]), solved)


def second_kernel(own, received, outer, inverse_high, inverse_low, outer_high, outer_low):
    outer_high[...], outer_low[...] = split(outer[:, 0:128])
    system = own[0:128, :] + received[0:128, :]
    inverse_high[...], inverse_low[...] = split(spd_inverse(system))


def assemble(alpha, beta):
    rows = (alpha or beta)[0].shape[0]
    left = halves((rows, 128))
    blank = jnp.zeros((rows, 128), F32)
    if alpha is None:
        tiles = (
            jnp.where(left, 0.0, turn(beta[0])),
            blank,
            jnp.where(left, 0.0, beta[0]),
            beta[1],
        )
        return jnp.concatenate(tiles, axis=1)
    turned = turn(alpha[1])
    middle = jnp.where(left, turn(alpha[0]), turned)
    if beta is None:
        tiles = jnp.where(left, alpha[0], 0.0), middle, jnp.where(left, turned, 0.0), blank
        return jnp.concatenate(tiles, axis=1)
    tiles = (
        jnp.where(left, alpha[0], turn(beta[0])),
        middle,
        jnp.where(left, turned, beta[0]),
        beta[1],
    )
    return jnp.concatenate(tiles, axis=1)


def exchange_kernel(
    place,
    own_one,
    own_two,
    received_one,
    received_two,
    link,
    inverse_high,
    inverse_low,
    message_one,
    message_two,
    right_high,
    right_low,
):
    is_alpha = place[0] == 0

    def both(mine, other):
        return jnp.where(is_alpha, mine, other), jnp.where(is_alpha, other, mine)

    def part(start, stop):
        return both(stacked(own_one, own_two, start, stop), stacked(received_one, received_two, start, stop))

    one, two = part(128, 256), part(256, 384)
    right = split(assemble((one[0], two[0]), (one[1], two[1])))
    face, back = part(384, 448), part(448, 512)
    direct = jnp.concatenate(
        [assemble((face[0], back[0]), None), assemble(None, (face[1], back[1]))], axis=0
    )
    mine = link[...]
    other = jnp.transpose(stacked(received_one, received_two, 128, 256))[0:FACE]
    coupling = jnp.concatenate(
        [jnp.where(is_alpha, mine, other), jnp.where(is_alpha, other, mine)], axis=0
    )
    solved = split(product(split(coupling), (inverse_high[...], inverse_low[...])))
    merged = direct - product(solved, right)
    for i in range(4):
        stack(message_one, message_two, 128 * i, merged[:, 128 * i : 128 * i + 128])
    right_high[...], right_low[...] = right


def rest_columns(one, two):
    return jnp.concatenate(
        [stacked(one, two, 128 * i, 128 * i + 128) for i in range(1, 4)], axis=1
    )


def outer_kernel(place, outer, outer_high, outer_low, inverse_high, inverse_low, right_high, right_low, rows):
    mine = outer[:, 128:256], outer[:, 256:384]
    direct = jnp.where(place[0] == 0, assemble(mine, None), assemble(None, mine))
    solved = split(product((outer_high[...], outer_low[...]), (inverse_high[...], inverse_low[...])))
    rows[...] = direct - product(solved, (right_high[...], right_low[...]))


def third_kernel(own_one, own_two, received, rows, half, solved_high, solved_low):
    right = split(rest_columns(own_one, own_two))
    system = own_one[0:128, :] + received[0:128, :]
    solved = split(spd_inverse(system, rows[:, 0:128]))
    half[...] = rows[:, 128:512] + product(solved, right)
    solved_high[...], solved_low[...] = solved


def last_kernel(
    place, half, received_one, received_two, solved_high, solved_low, out, other, sems
):
    third = place[1]
    width = 6 * FACE

    def copy(source, side, start, i):
        first = pl.multiple_of(side * width + start, 128)
        target = out.at[:, pl.ds(first, source.shape[1])]
        return pltpu.make_async_copy(source, target, sems.at[i])

    copies = [copy(half, third, 0, 0)]
    copies[0].start()
    solved = solved_high[...], solved_low[...]
    for i in range(3):
        right = split(stacked(received_one, received_two, 128 * i + 128, 128 * i + 256))
        other[i] = product(solved, right)
        copies.append(copy(other.at[i], 1 - third, 128 * i, i + 1))
        copies[-1].start()
    for x in copies:
        x.wait()


def shapes(*sizes):
    return [jax.ShapeDtypeStruct(size, F32) for size in sizes]


def pair(*size):
    return [jax.ShapeDtypeStruct(size, BF16)] * 2


def run(kernel, out_shape, *operands, scalars=1, out_space=pltpu.VMEM, **options):
    smem = pl.BlockSpec(memory_space=pltpu.SMEM)
    vmem = pl.BlockSpec(memory_space=pltpu.VMEM)
    return pl.pallas_call(
        kernel,
        out_shape=out_shape,
        in_specs=[smem] * scalars + [vmem] * (len(operands) - scalars),
        out_specs=[pl.BlockSpec(memory_space=out_space)] * len(out_shape),
        compiler_params=pltpu.CompilerParams(vmem_limit_bytes=32 * 1024 * 1024),
        **options,
    )(*operands)


def body(leaf_maps, leaf_operator, region_eps, wave_sq, region_labels, build_flags):
    across = lax.axis_index("bx") % 2
    upward = lax.axis_index("by")
    place = jnp.stack([across, upward // 2 % 2, upward % 2]).astype(jnp.int32)
    size = leaf_operator.shape[0]
    mine = pl.pallas_call(
        build_kernel,
        out_shape=jax.ShapeDtypeStruct((LEAF, LEAF), F32),
        in_specs=[pl.BlockSpec(memory_space=pltpu.SMEM)] * 3
        + [pl.BlockSpec(memory_space=pltpu.HBM)] * 3,
        out_specs=pl.BlockSpec(memory_space=pltpu.VMEM),
        scratch_shapes=[
            pltpu.VMEM(region_eps.shape, F32),
            pltpu.VMEM((128, size), F32),
            pltpu.VMEM((size - LEAF - 128, size), F32),
            pltpu.VMEM((LEAF, size), F32),
            pltpu.SemaphoreType.DMA((5,)),
        ],
        compiler_params=pltpu.CompilerParams(vmem_limit_bytes=32 * 1024 * 1024),
        name="leaf_build",
    )(
        region_labels,
        build_flags,
        wave_sq,
        *(
            pltpu.with_memory_space_constraint(x, pltpu.HBM)
            for x in (leaf_maps[0, 0], leaf_operator, region_eps)
        ),
    )
    theirs = swapped(mine, "by", 0)
    one, two, link, *solved = run(
        first_kernel,
        shapes((CUT_TWO, 128), (512 - CUT_TWO, 128), (FACE, 128)) + pair(FACE, 6 * FACE),
        place,
        mine,
        theirs,
        name="first_merge",
    )
    received_one = swapped(one, "bx", 0)
    received_two = swapped(two, "bx", 0)
    (outer,) = run(
        rows_kernel,
        shapes((96, 6 * FACE)),
        place,
        mine,
        theirs,
        *solved,
        scratch_shapes=[pltpu.VMEM((192, 6 * FACE), F32), pltpu.VMEM((192, 128), F32)],
        name="first_rows",
    )
    *inverse, outer_high, outer_low = run(
        second_kernel,
        pair(128, 128) + pair(96, 128),
        one,
        received_one,
        outer,
        scalars=0,
        cost_estimate=LONG,
        name="second_inverse",
    )
    one, two, *right = run(
        exchange_kernel,
        shapes((CUT_THREE, 128), (512 - CUT_THREE, 128)) + pair(128, 8 * FACE),
        place,
        one,
        two,
        received_one,
        received_two,
        link,
        *inverse,
        name="second_merge",
    )
    received_one = swapped(one, "by", 1)
    received_two = swapped(two, "by", 1)
    (rows,) = run(
        outer_kernel,
        shapes((96, 8 * FACE)),
        place,
        outer,
        outer_high,
        outer_low,
        *inverse,
        *right,
        name="second_rows",
    )
    half, *solved = run(
        third_kernel,
        shapes((96, 6 * FACE)) + pair(96, 128),
        one,
        two,
        received_one,
        rows,
        scalars=0,
        cost_estimate=LONG,
        name="third_inverse",
    )
    (result,) = run(
        last_kernel,
        shapes((96, 12 * FACE)),
        place,
        half,
        received_one,
        received_two,
        *solved,
        scratch_shapes=[pltpu.VMEM((3, 96, 128), F32), pltpu.SemaphoreType.DMA((4,))],
        out_space=pltpu.HBM,
        name="third_merge",
    )
    return result.reshape((1, 1, 96, 12 * FACE))


def solution(mesh):
    placed = (
        P(("freq", "bx"), "by", None, None),
        P(),
        P(),
        P("freq"),
        P("bx", "by"),
        P("bx", "by"),
    )
    return jax.shard_map(
        body,
        mesh=mesh,
        in_specs=placed,
        out_specs=P(("freq", "bx"), "by", None, None),
        check_vma=False,
    )
```

profile of v0, /device:TPU:6, one launch (start us, length us, event | category | flops | bytes accessed | tf_op | source)
XLA Modules:
  0.0 39.2 jit_solution(872985317530702008)
XLA Ops:
  1.9 1.0 %leaf_build.1.mine = f32[256,256]{1,0:T(8,128)S(1)} custom-call(s32[1,1]{1,0:T(1,128)S(6)} %copy.8.label, s32[1,1]{1,0:T(1,128)S(6)} %copy.9.flag, f32[1]{0:T(128)S(6)} %copy.7.wave, f32[256,256]{1,0:T(8,128)} %bitcast.5, f32[472,472]{1,0:T(8,128)} %operator.1, f32[8,472]{1,0:T(8,128)} %table_at.1), custom_call_target="tpu_custom_call" | custom-call | tf_op jit(solution)/shard_map/leaf_build/pallas_call | solution.py:464
  2.9 1.9 %collective-permute-start = (f32[256,256]{1,0:T(8,128)S(1)}, f32[256,256]{1,0:T(8,128)S(1)}, u32[]{:S(2)}, u32[]{:S(2)}) collective-permute-start(f32[256,256]{1,0:T(8,128)S(1)} %leaf_build.1.mine), channel_id=1, source_target_pairs={{0,4},{4,0},{8,12},{12,8},{16,20},{20,16},{24,28},{28,24},{32,36},... | collective-permute-start | bytes 786440 | tf_op jit(solution)/shard_map/ppermute | solution.py:19
  4.9 0.1 pad_add_fusion.place
  5.0 1.4 %collective-permute-done.theirs = f32[256,256]{1,0:T(8,128)S(1)} collective-permute-done((f32[256,256]{1,0:T(8,128)S(1)}, f32[256,256]{1,0:T(8,128)S(1)}, u32[]{:S(2)}, u32[]{:S(2)}) %collective-permute-start) | collective-permute-done | bytes 262176 | tf_op jit(solution)/shard_map/ppermute | solution.py:19
  6.4 2.2 %first_merge.1 = (f32[200,128]{1,0:T(8,128)S(1)}, f32[312,128]{1,0:T(8,128)S(1)}, f32[64,128]{1,0:T(8,128)S(1)}, bf16[64,384]{1,0:T(8,128)(2,1)S(1)}, bf16[64,384]{1,0:T(8,128)(2,1)S(1)}) custom-call(s32[3]{0:T(128)S(1)} %pad_add_fusion.place, f32[256,256]{1,0:T(8,128)S(1)} %leaf_build.1.mine, f32[256,256]{1,0:T(8,128)S(1)} %collective-permute-done.theirs), custom_call_target="tpu_custom_call" | custom-call | tf_op jit(solution)/shard_map/first_merge/pallas_call | solution.py:449
  8.5 4.3 %collective-permute-start.1 = (f32[200,128]{1,0:T(8,128)S(1)}, f32[200,128]{1,0:T(8,128)S(1)}, u32[]{:S(2)}, u32[]{:S(2)}) collective-permute-start(f32[200,128]{1,0:T(8,128)S(1)} %get-tuple-element.21.own.own_one), channel_id=1, source_target_pairs={{0,64},{64,0},{128,192},{192,128},{256,320},{320,256},{384,448},{4... | collective-permute-start | bytes 307208 | tf_op jit(solution)/shard_map/ppermute | solution.py:19
  12.8 1.9 %collective-permute-start.2 = (f32[312,128]{1,0:T(8,128)S(1)}, f32[312,128]{1,0:T(8,128)S(1)}, u32[]{:S(2)}, u32[]{:S(2)}) collective-permute-start(f32[312,128]{1,0:T(8,128)S(1)} %get-tuple-element.22.own_two), channel_id=1, source_target_pairs={{0,64},{64,0},{128,192},{192,128},{256,320},{320,256},{384,448},{4... | collective-permute-start | bytes 479240 | tf_op jit(solution)/shard_map/ppermute | solution.py:19
  14.8 0.9 %first_rows.1.outer = f32[96,384]{1,0:T(8,128)S(1)} custom-call(s32[3]{0:T(128)S(1)} %pad_add_fusion.place, f32[256,256]{1,0:T(8,128)S(1)} %leaf_build.1.mine, f32[256,256]{1,0:T(8,128)S(1)} %collective-permute-done.theirs, bf16[64,384]{1,0:T(8,128)(2,1)S(1)} %get-tuple-element.24.solved_high, bf16[64,384]{1,0:T(8,128)(2,1)S(1)} %get-tuple-element.25.solved_low), custom_call_target="tpu_custom_call" | custom-call | tf_op jit(solution)/shard_map/first_rows/pallas_call | solution.py:449
  15.6 0.4 collective-permute-done.1.received.received_one
  16.0 2.6 %second_inverse.1 = (bf16[128,128]{1,0:T(8,128)(2,1)S(1)}, bf16[128,128]{1,0:T(8,128)(2,1)S(1)}, bf16[96,128]{1,0:T(8,128)(2,1)S(1)}, bf16[96,128]{1,0:T(8,128)(2,1)S(1)}) custom-call(f32[200,128]{1,0:T(8,128)S(1)} %get-tuple-element.21.own.own_one, f32[200,128]{1,0:T(8,128)S(1)} %collective-permute-done.1.received.received_one, f32[96,384]{1,0:T(8,128)S(1)} %first_rows.1.outer), custom_call_target="tpu_custom_call" | custom-call | flops 10000000000 | bytes 100000000 | tf_op jit(solution)/shard_map/second_inverse/pallas_call | solution.py:449
  18.6 2.0 %collective-permute-done.2.received_two = f32[312,128]{1,0:T(8,128)S(1)} collective-permute-done((f32[312,128]{1,0:T(8,128)S(1)}, f32[312,128]{1,0:T(8,128)S(1)}, u32[]{:S(2)}, u32[]{:S(2)}) %collective-permute-start.2) | collective-permute-done | bytes 159776 | tf_op jit(solution)/shard_map/ppermute | solution.py:19
  20.6 0.9 %second_merge.1 = (f32[160,128]{1,0:T(8,128)S(1)}, f32[352,128]{1,0:T(8,128)S(1)}, bf16[128,512]{1,0:T(8,128)(2,1)S(1)}, bf16[128,512]{1,0:T(8,128)(2,1)S(1)}) custom-call(s32[3]{0:T(128)S(1)} %pad_add_fusion.place, f32[200,128]{1,0:T(8,128)S(1)} %get-tuple-element.21.own.own_one, f32[312,128]{1,0:T(8,128)S(1)} %get-tuple-element.22.own_two, ...), custom_call_target="tpu_custom_call" | custom-call | tf_op jit(solution)/shard_map/second_merge/pallas_call | solution.py:449
  21.6 8.9 %collective-permute-start.3 = (f32[160,128]{1,0:T(8,128)S(1)}, f32[160,128]{1,0:T(8,128)S(1)}, u32[]{:S(2)}, u32[]{:S(2)}) collective-permute-start(f32[160,128]{1,0:T(8,128)S(1)} %get-tuple-element.28.own_one), channel_id=1, source_target_pairs={{0,8},{4,12},{8,0},{12,4},{16,24},{20,28},{24,16},{28,20},{32,40},... | collective-permute-start | bytes 245768 | tf_op jit(solution)/shard_map/ppermute | solution.py:19
  30.4 1.9 %collective-permute-start.4 = (f32[352,128]{1,0:T(8,128)S(1)}, f32[352,128]{1,0:T(8,128)S(1)}, u32[]{:S(2)}, u32[]{:S(2)}) collective-permute-start(f32[352,128]{1,0:T(8,128)S(1)} %get-tuple-element.29.own_two), channel_id=1, source_target_pairs={{0,8},{4,12},{8,0},{12,4},{16,24},{20,28},{24,16},{28,20},{32,40},... | collective-permute-start | bytes 540680 | tf_op jit(solution)/shard_map/ppermute | solution.py:19
  32.3 0.9 %second_rows.1.rows = f32[96,512]{1,0:T(8,128)S(1)} custom-call(s32[3]{0:T(128)S(1)} %pad_add_fusion.place, f32[96,384]{1,0:T(8,128)S(1)} %first_rows.1.outer, bf16[96,128]{1,0:T(8,128)(2,1)S(1)} %get-tuple-element.30.outer_high, bf16[96,128]{1,0:T(8,128)(2,1)S(1)} %get-tuple-element.31.outer_low, bf16[128,128]{1,0:T(8,128)(2,1)S(1)} %get-tuple-element.26.inverse_high, ...), custom_call_target="tpu_custom_call" | custom-call | tf_op jit(solution)/shard_map/second_rows/pallas_call | solution.py:449
  33.2 0.0 collective-permute-done.3.received.received_one
  33.2 2.8 %third_inverse.1 = (f32[96,384]{1,0:T(8,128)S(1)}, bf16[96,128]{1,0:T(8,128)(2,1)S(1)}, bf16[96,128]{1,0:T(8,128)(2,1)S(1)}) custom-call(f32[160,128]{1,0:T(8,128)S(1)} %get-tuple-element.28.own_one, f32[352,128]{1,0:T(8,128)S(1)} %get-tuple-element.29.own_two, f32[160,128]{1,0:T(8,128)S(1)} %collective-permute-done.3.received.received_one, ...), custom_call_target="tpu_custom_call" | custom-call | flops 10000000000 | bytes 100000000 | tf_op jit(solution)/shard_map/third_inverse/pallas_call | solution.py:449
  36.1 1.7 %collective-permute-done.4.received_two = f32[352,128]{1,0:T(8,128)S(1)} collective-permute-done((f32[352,128]{1,0:T(8,128)S(1)}, f32[352,128]{1,0:T(8,128)S(1)}, u32[]{:S(2)}, u32[]{:S(2)}) %collective-permute-start.4) | collective-permute-done | bytes 180256 | tf_op jit(solution)/shard_map/ppermute | solution.py:19
  37.8 1.4 %third_merge.1 = f32[96,768]{1,0:T(8,128)} custom-call(s32[3]{0:T(128)S(1)} %pad_add_fusion.place, f32[96,384]{1,0:T(8,128)S(1)} %get-tuple-element.34.half, f32[160,128]{1,0:T(8,128)S(1)} %collective-permute-done.3.received.received_one, f32[352,128]{1,0:T(8,128)S(1)} %collective-permute-done.4.received_two, ...), custom_call_target="tpu_custom_call" | custom-call | tf_op jit(solution)/shard_map/third_merge/pallas_call | solution.py:449
Async XLA Ops:
  2.9 3.4 %collective-permute-start = (f32[256,256]{1,0:T(8,128)S(1)}, f32[256,256]{1,0:T(8,128)S(1)}, u32[]{:S(2)}, u32[]{:S(2)}) collective-permute-start(f32[256,256]{1,0:T(8,128)S(1)} %leaf_build.1.mine), channel_id=1, source_target_pairs={{0,4},{4,0},{8,12},{12,8},{16,20},{20,16},{24,28},{28,24},{32,36},... | collective-permute-start | bytes 786440 | tf_op jit(solution)/shard_map/ppermute | solution.py:19
  8.5 7.5 %collective-permute-start.1 = (f32[200,128]{1,0:T(8,128)S(1)}, f32[200,128]{1,0:T(8,128)S(1)}, u32[]{:S(2)}, u32[]{:S(2)}) collective-permute-start(f32[200,128]{1,0:T(8,128)S(1)} %get-tuple-element.21.own.own_one), channel_id=1, source_target_pairs={{0,64},{64,0},{128,192},{192,128},{256,320},{320,256},{384,448},{4... | collective-permute-start | bytes 307208 | tf_op jit(solution)/shard_map/ppermute | solution.py:19
  12.8 7.8 %collective-permute-start.2 = (f32[312,128]{1,0:T(8,128)S(1)}, f32[312,128]{1,0:T(8,128)S(1)}, u32[]{:S(2)}, u32[]{:S(2)}) collective-permute-start(f32[312,128]{1,0:T(8,128)S(1)} %get-tuple-element.22.own_two), channel_id=1, source_target_pairs={{0,64},{64,0},{128,192},{192,128},{256,320},{320,256},{384,448},{4... | collective-permute-start | bytes 479240 | tf_op jit(solution)/shard_map/ppermute | solution.py:19
  21.6 11.7 %collective-permute-start.3 = (f32[160,128]{1,0:T(8,128)S(1)}, f32[160,128]{1,0:T(8,128)S(1)}, u32[]{:S(2)}, u32[]{:S(2)}) collective-permute-start(f32[160,128]{1,0:T(8,128)S(1)} %get-tuple-element.28.own_one), channel_id=1, source_target_pairs={{0,8},{4,12},{8,0},{12,4},{16,24},{20,28},{24,16},{28,20},{32,40},... | collective-permute-start | bytes 245768 | tf_op jit(solution)/shard_map/ppermute | solution.py:19
  30.4 7.4 %collective-permute-start.4 = (f32[352,128]{1,0:T(8,128)S(1)}, f32[352,128]{1,0:T(8,128)S(1)}, u32[]{:S(2)}, u32[]{:S(2)}) collective-permute-start(f32[352,128]{1,0:T(8,128)S(1)} %get-tuple-element.29.own_two), channel_id=1, source_target_pairs={{0,8},{4,12},{8,0},{12,4},{16,24},{20,28},{24,16},{28,20},{32,40},... | collective-permute-start | bytes 540680 | tf_op jit(solution)/shard_map/ppermute | solution.py:19
where the time goes:
time: 39.5 us; the launch traced here: 39.2 us
  starting transfers between devices  18.9 us (48%)
  Pallas kernels  12.7 us (32%)
  waiting for transfers between devices  5.48 us (14%)
  between operations  2.07 us (5%)
    ppermute x5, starting transfers between devices, swapped(): lax.ppermute(shard, axis, [(i, i ^ 1 << stride) for i in range(lax.axis_s...  18.9 us
    pallas_call x7, Pallas kernels, run(): pl.pallas_call(kernel, out_shape=out_shape, in_specs=[smem] * scalars + [...  11.7 us
    ppermute x5, waiting for transfers between devices, swapped(): lax.ppermute(shard, axis, [(i, i ^ 1 << stride) for i in range(lax.axis_s...  5.48 us
    pallas_call x1, Pallas kernels, body(): pl.pallas_call(build_kernel, out_shape=jax.ShapeDtypeStruct((LEAF, LEAF),...  1 us
  transfers between devices with their start and end apart: 5, of which 4 were waited for; matrix products, arithmetic and copies ran while one was open for 0% of the time, Pallas kernels for 18%

commit v1 on v0

--- a/solution.py
+++ b/solution.py
@@ -7,7 +7,8 @@
 
 FACE = 64
 LEAF = 4 * FACE
-CUT_TWO, CUT_THREE = 200, 160
+MESSAGE = 96 + 3 * 128
+CUT_TWO, CUT_THREE = 184, 144
 F32 = jnp.float32
 BF16 = jnp.bfloat16
 
@@ -264,6 +265,18 @@
     return [jnp.where(flag, x, y) for x, y in zip(one, other)]
 
 
+def packed(system):
+    low = jnp.where(halves((32, 128)), turn(system[64:96]), system[96:128])
+    return jnp.concatenate([system[0:64], low], axis=0)
+
+
+def unpacked(parts):
+    top, low = parts[0:64], parts[64:96]
+    across = jnp.transpose(jnp.concatenate([top, top], axis=0))[64:128]
+    corner = jnp.concatenate([turn(low), low], axis=0)
+    return jnp.concatenate([top, jnp.where(halves((64, 128)), across, corner)], axis=0)
+
+
 def stacked(one, two, start, stop):
     cut = one.shape[0]
     parts = []
@@ -296,10 +309,11 @@
     inverse = split(spd_inverse(system, panel=8))
     solved = split(product(inverse, right))
     merged = direct - product(coupling, solved)
-    for i in range(3):
-        stack(message_one, message_two, 128 * i, merged[0:128, 128 * i : 128 * i + 128])
-    stack(message_one, message_two, 384, merged[128:192, 128:256])
-    stack(message_one, message_two, 448, merged[128:192, 256:384])
+    stack(message_one, message_two, 0, packed(merged[0:128, 0:128]))
+    stack(message_one, message_two, 96, merged[0:128, 128:256])
+    stack(message_one, message_two, 224, merged[0:128, 256:384])
+    stack(message_one, message_two, 352, merged[128:192, 128:256])
+    stack(message_one, message_two, 416, merged[128:192, 256:384])
     link[...] = merged[128:192, 0:128]
     solved_high[...], solved_low[...] = solved
 
@@ -321,7 +335,7 @@
 
 def second_kernel(own, received, outer, inverse_high, inverse_low, outer_high, outer_low):
     outer_high[...], outer_low[...] = split(outer[:, 0:128])
-    system = own[0:128, :] + received[0:128, :]
+    system = unpacked(own[0:96, :] + received[0:96, :])
     inverse_high[...], inverse_low[...] = split(spd_inverse(system))
 
 
@@ -373,27 +387,28 @@
     def part(start, stop):
         return both(stacked(own_one, own_two, start, stop), stacked(received_one, received_two, start, stop))
 
-    one, two = part(128, 256), part(256, 384)
+    one, two = part(96, 224), part(224, 352)
     right = split(assemble((one[0], two[0]), (one[1], two[1])))
-    face, back = part(384, 448), part(448, 512)
+    face, back = part(352, 416), part(416, 480)
     direct = jnp.concatenate(
         [assemble((face[0], back[0]), None), assemble(None, (face[1], back[1]))], axis=0
     )
     mine = link[...]
-    other = jnp.transpose(stacked(received_one, received_two, 128, 256))[0:FACE]
+    other = jnp.transpose(stacked(received_one, received_two, 96, 224))[0:FACE]
     coupling = jnp.concatenate(
         [jnp.where(is_alpha, mine, other), jnp.where(is_alpha, other, mine)], axis=0
     )
     solved = split(product(split(coupling), (inverse_high[...], inverse_low[...])))
     merged = direct - product(solved, right)
-    for i in range(4):
-        stack(message_one, message_two, 128 * i, merged[:, 128 * i : 128 * i + 128])
+    stack(message_one, message_two, 0, packed(merged[:, 0:128]))
+    for i in range(3):
+        stack(message_one, message_two, 96 + 128 * i, merged[:, 128 * i + 128 : 128 * i + 256])
     right_high[...], right_low[...] = right
 
 
 def rest_columns(one, two):
     return jnp.concatenate(
-        [stacked(one, two, 128 * i, 128 * i + 128) for i in range(1, 4)], axis=1
+        [stacked(one, two, 128 * i + 96, 128 * i + 224) for i in range(3)], axis=1
     )
 
 
@@ -406,7 +421,7 @@
 
 def third_kernel(own_one, own_two, received, rows, half, solved_high, solved_low):
     right = split(rest_columns(own_one, own_two))
-    system = own_one[0:128, :] + received[0:128, :]
+    system = unpacked(own_one[0:96, :] + received[0:96, :])
     solved = split(spd_inverse(system, rows[:, 0:128]))
     half[...] = rows[:, 128:512] + product(solved, right)
     solved_high[...], solved_low[...] = solved
@@ -427,7 +442,7 @@
     copies[0].start()
     solved = solved_high[...], solved_low[...]
     for i in range(3):
-        right = split(stacked(received_one, received_two, 128 * i + 128, 128 * i + 256))
+        right = split(stacked(received_one, received_two, 128 * i + 96, 128 * i + 224))
         other[i] = product(solved, right)
         copies.append(copy(other.at[i], 1 - third, 128 * i, i + 1))
         copies[-1].start()
@@ -488,7 +503,7 @@
     theirs = swapped(mine, "by", 0)
     one, two, link, *solved = run(
         first_kernel,
-        shapes((CUT_TWO, 128), (512 - CUT_TWO, 128), (FACE, 128)) + pair(FACE, 6 * FACE),
+        shapes((CUT_TWO, 128), (MESSAGE - CUT_TWO, 128), (FACE, 128)) + pair(FACE, 6 * FACE),
         place,
         mine,
         theirs,
@@ -518,7 +533,7 @@
     )
     one, two, *right = run(
         exchange_kernel,
-        shapes((CUT_THREE, 128), (512 - CUT_THREE, 128)) + pair(128, 8 * FACE),
+        shapes((CUT_THREE, 128), (MESSAGE - CUT_THREE, 128)) + pair(128, 8 * FACE),
         place,
         one,
         two,

time: 39.5 us -> 39 us (0.987)
  the two profiles are of different devices: /device:TPU:6 before, /device:TPU:18 now
where the time goes in v1:
time: 39 us; the launch traced here: 38.7 us
  starting transfers between devices  20.4 us (52%)
  Pallas kernels  12.9 us (33%)
  waiting for transfers between devices  3.38 us (9%)
  between operations  2.06 us (5%)
    ppermute x5, starting transfers between devices, swapped(): lax.ppermute(shard, axis, [(i, i ^ 1 << stride) for i in range(lax.axis_s...  20.4 us
    pallas_call x7, Pallas kernels, run(): pl.pallas_call(kernel, out_shape=out_shape, in_specs=[smem] * scalars + [...  11.9 us
    ppermute x5, waiting for transfers between devices, swapped(): lax.ppermute(shard, axis, [(i, i ^ 1 << stride) for i in range(lax.axis_s...  3.38 us
    pallas_call x1, Pallas kernels, body(): pl.pallas_call(build_kernel, out_shape=jax.ShapeDtypeStruct((LEAF, LEAF),...  1 us
  transfers between devices with their start and end apart: 5, of which 4 were waited for; matrix products, arithmetic and copies ran while one was open for 0% of the time, Pallas kernels for 19%

profile of v1, /device:TPU:18, one launch (start us, length us, event | category | flops | bytes accessed | tf_op | source)
XLA Modules:
  0.0 38.7 jit_solution(7527108466675603828)
XLA Ops:
  1.9 1.0 %leaf_build.1.mine = f32[256,256]{1,0:T(8,128)S(1)} custom-call(s32[1,1]{1,0:T(1,128)S(6)} %copy.8.label, s32[1,1]{1,0:T(1,128)S(6)} %copy.9.flag, f32[1]{0:T(128)S(6)} %copy.7.wave, f32[256,256]{1,0:T(8,128)} %bitcast.5, f32[472,472]{1,0:T(8,128)} %operator.1, f32[8,472]{1,0:T(8,128)} %table_at.1), custom_call_target="tpu_custom_call" | custom-call | tf_op jit(solution)/shard_map/leaf_build/pallas_call | solution.py:479
  2.9 7.1 %collective-permute-start = (f32[256,256]{1,0:T(8,128)S(1)}, f32[256,256]{1,0:T(8,128)S(1)}, u32[]{:S(2)}, u32[]{:S(2)}) collective-permute-start(f32[256,256]{1,0:T(8,128)S(1)} %leaf_build.1.mine), channel_id=1, source_target_pairs={{0,4},{4,0},{8,12},{12,8},{16,20},{20,16},{24,28},{28,24},{32,36},... | collective-permute-start | bytes 786440 | tf_op jit(solution)/shard_map/ppermute | solution.py:20
  10.1 0.1 pad_add_fusion.place
  10.2 1.0 %collective-permute-done.theirs = f32[256,256]{1,0:T(8,128)S(1)} collective-permute-done((f32[256,256]{1,0:T(8,128)S(1)}, f32[256,256]{1,0:T(8,128)S(1)}, u32[]{:S(2)}, u32[]{:S(2)}) %collective-permute-start) | collective-permute-done | bytes 262176 | tf_op jit(solution)/shard_map/ppermute | solution.py:20
  11.2 2.2 %first_merge.1 = (f32[184,128]{1,0:T(8,128)S(1)}, f32[296,128]{1,0:T(8,128)S(1)}, f32[64,128]{1,0:T(8,128)S(1)}, bf16[64,384]{1,0:T(8,128)(2,1)S(1)}, bf16[64,384]{1,0:T(8,128)(2,1)S(1)}) custom-call(s32[3]{0:T(128)S(1)} %pad_add_fusion.place, f32[256,256]{1,0:T(8,128)S(1)} %leaf_build.1.mine, f32[256,256]{1,0:T(8,128)S(1)} %collective-permute-done.theirs), custom_call_target="tpu_custom_call" | custom-call | tf_op jit(solution)/shard_map/first_merge/pallas_call | solution.py:464
  13.4 1.9 %collective-permute-start.1 = (f32[184,128]{1,0:T(8,128)S(1)}, f32[184,128]{1,0:T(8,128)S(1)}, u32[]{:S(2)}, u32[]{:S(2)}) collective-permute-start(f32[184,128]{1,0:T(8,128)S(1)} %get-tuple-element.21.own.own_one), channel_id=1, source_target_pairs={{0,64},{64,0},{128,192},{192,128},{256,320},{320,256},{384,448},{4... | collective-permute-start | bytes 282632 | tf_op jit(solution)/shard_map/ppermute | solution.py:20
  15.3 3.9 %collective-permute-start.2 = (f32[296,128]{1,0:T(8,128)S(1)}, f32[296,128]{1,0:T(8,128)S(1)}, u32[]{:S(2)}, u32[]{:S(2)}) collective-permute-start(f32[296,128]{1,0:T(8,128)S(1)} %get-tuple-element.22.own_two), channel_id=1, source_target_pairs={{0,64},{64,0},{128,192},{192,128},{256,320},{320,256},{384,448},{4... | collective-permute-start | bytes 454664 | tf_op jit(solution)/shard_map/ppermute | solution.py:20
  19.3 0.9 %first_rows.1.outer = f32[96,384]{1,0:T(8,128)S(1)} custom-call(s32[3]{0:T(128)S(1)} %pad_add_fusion.place, f32[256,256]{1,0:T(8,128)S(1)} %leaf_build.1.mine, f32[256,256]{1,0:T(8,128)S(1)} %collective-permute-done.theirs, bf16[64,384]{1,0:T(8,128)(2,1)S(1)} %get-tuple-element.24.solved_high, bf16[64,384]{1,0:T(8,128)(2,1)S(1)} %get-tuple-element.25.solved_low), custom_call_target="tpu_custom_call" | custom-call | tf_op jit(solution)/shard_map/first_rows/pallas_call | solution.py:464
  20.2 0.2 collective-permute-done.1.received.received_one
  20.3 2.6 %second_inverse.1 = (bf16[128,128]{1,0:T(8,128)(2,1)S(1)}, bf16[128,128]{1,0:T(8,128)(2,1)S(1)}, bf16[96,128]{1,0:T(8,128)(2,1)S(1)}, bf16[96,128]{1,0:T(8,128)(2,1)S(1)}) custom-call(f32[184,128]{1,0:T(8,128)S(1)} %get-tuple-element.21.own.own_one, f32[184,128]{1,0:T(8,128)S(1)} %collective-permute-done.1.received.received_one, f32[96,384]{1,0:T(8,128)S(1)} %first_rows.1.outer), custom_call_target="tpu_custom_call" | custom-call | flops 10000000000 | bytes 100000000 | tf_op jit(solution)/shard_map/second_inverse/pallas_call | solution.py:464
  23.0 0.6 %collective-permute-done.2.received_two = f32[296,128]{1,0:T(8,128)S(1)} collective-permute-done((f32[296,128]{1,0:T(8,128)S(1)}, f32[296,128]{1,0:T(8,128)S(1)}, u32[]{:S(2)}, u32[]{:S(2)}) %collective-permute-start.2) | collective-permute-done | bytes 151584 | tf_op jit(solution)/shard_map/ppermute | solution.py:20
  23.5 1.0 %second_merge.1 = (f32[144,128]{1,0:T(8,128)S(1)}, f32[336,128]{1,0:T(8,128)S(1)}, bf16[128,512]{1,0:T(8,128)(2,1)S(1)}, bf16[128,512]{1,0:T(8,128)(2,1)S(1)}) custom-call(s32[3]{0:T(128)S(1)} %pad_add_fusion.place, f32[184,128]{1,0:T(8,128)S(1)} %get-tuple-element.21.own.own_one, f32[296,128]{1,0:T(8,128)S(1)} %get-tuple-element.22.own_two, ...), custom_call_target="tpu_custom_call" | custom-call | tf_op jit(solution)/shard_map/second_merge/pallas_call | solution.py:464
  24.5 5.5 %collective-permute-start.3 = (f32[144,128]{1,0:T(8,128)S(1)}, f32[144,128]{1,0:T(8,128)S(1)}, u32[]{:S(2)}, u32[]{:S(2)}) collective-permute-start(f32[144,128]{1,0:T(8,128)S(1)} %get-tuple-element.28.own_one), channel_id=1, source_target_pairs={{0,8},{4,12},{8,0},{12,4},{16,24},{20,28},{24,16},{28,20},{32,40},... | collective-permute-start | bytes 221192 | tf_op jit(solution)/shard_map/ppermute | solution.py:20
  30.0 1.9 %collective-permute-start.4 = (f32[336,128]{1,0:T(8,128)S(1)}, f32[336,128]{1,0:T(8,128)S(1)}, u32[]{:S(2)}, u32[]{:S(2)}) collective-permute-start(f32[336,128]{1,0:T(8,128)S(1)} %get-tuple-element.29.own_two), channel_id=1, source_target_pairs={{0,8},{4,12},{8,0},{12,4},{16,24},{20,28},{24,16},{28,20},{32,40},... | collective-permute-start | bytes 516104 | tf_op jit(solution)/shard_map/ppermute | solution.py:20
  31.9 0.9 %second_rows.1.rows = f32[96,512]{1,0:T(8,128)S(1)} custom-call(s32[3]{0:T(128)S(1)} %pad_add_fusion.place, f32[96,384]{1,0:T(8,128)S(1)} %first_rows.1.outer, bf16[96,128]{1,0:T(8,128)(2,1)S(1)} %get-tuple-element.30.outer_high, bf16[96,128]{1,0:T(8,128)(2,1)S(1)} %get-tuple-element.31.outer_low, bf16[128,128]{1,0:T(8,128)(2,1)S(1)} %get-tuple-element.26.inverse_high, ...), custom_call_target="tpu_custom_call" | custom-call | tf_op jit(solution)/shard_map/second_rows/pallas_call | solution.py:464
  32.8 0.0 collective-permute-done.3.received.received_one
  32.8 2.9 %third_inverse.1 = (f32[96,384]{1,0:T(8,128)S(1)}, bf16[96,128]{1,0:T(8,128)(2,1)S(1)}, bf16[96,128]{1,0:T(8,128)(2,1)S(1)}) custom-call(f32[144,128]{1,0:T(8,128)S(1)} %get-tuple-element.28.own_one, f32[336,128]{1,0:T(8,128)S(1)} %get-tuple-element.29.own_two, f32[144,128]{1,0:T(8,128)S(1)} %collective-permute-done.3.received.received_one, ...), custom_call_target="tpu_custom_call" | custom-call | flops 10000000000 | bytes 100000000 | tf_op jit(solution)/shard_map/third_inverse/pallas_call | solution.py:464
  35.7 1.6 %collective-permute-done.4.received_two = f32[336,128]{1,0:T(8,128)S(1)} collective-permute-done((f32[336,128]{1,0:T(8,128)S(1)}, f32[336,128]{1,0:T(8,128)S(1)}, u32[]{:S(2)}, u32[]{:S(2)}) %collective-permute-start.4) | collective-permute-done | bytes 172064 | tf_op jit(solution)/shard_map/ppermute | solution.py:20
  37.3 1.4 %third_merge.1 = f32[96,768]{1,0:T(8,128)} custom-call(s32[3]{0:T(128)S(1)} %pad_add_fusion.place, f32[96,384]{1,0:T(8,128)S(1)} %get-tuple-element.34.half, f32[144,128]{1,0:T(8,128)S(1)} %collective-permute-done.3.received.received_one, f32[336,128]{1,0:T(8,128)S(1)} %collective-permute-done.4.received_two, ...), custom_call_target="tpu_custom_call" | custom-call | tf_op jit(solution)/shard_map/third_merge/pallas_call | solution.py:464
Async XLA Ops:
  2.9 8.3 %collective-permute-start = (f32[256,256]{1,0:T(8,128)S(1)}, f32[256,256]{1,0:T(8,128)S(1)}, u32[]{:S(2)}, u32[]{:S(2)}) collective-permute-start(f32[256,256]{1,0:T(8,128)S(1)} %leaf_build.1.mine), channel_id=1, source_target_pairs={{0,4},{4,0},{8,12},{12,8},{16,20},{20,16},{24,28},{28,24},{32,36},... | collective-permute-start | bytes 786440 | tf_op jit(solution)/shard_map/ppermute | solution.py:20
  13.4 6.9 %collective-permute-start.1 = (f32[184,128]{1,0:T(8,128)S(1)}, f32[184,128]{1,0:T(8,128)S(1)}, u32[]{:S(2)}, u32[]{:S(2)}) collective-permute-start(f32[184,128]{1,0:T(8,128)S(1)} %get-tuple-element.21.own.own_one), channel_id=1, source_target_pairs={{0,64},{64,0},{128,192},{192,128},{256,320},{320,256},{384,448},{4... | collective-permute-start | bytes 282632 | tf_op jit(solution)/shard_map/ppermute | solution.py:20
  15.3 8.2 %collective-permute-start.2 = (f32[296,128]{1,0:T(8,128)S(1)}, f32[296,128]{1,0:T(8,128)S(1)}, u32[]{:S(2)}, u32[]{:S(2)}) collective-permute-start(f32[296,128]{1,0:T(8,128)S(1)} %get-tuple-element.22.own_two), channel_id=1, source_target_pairs={{0,64},{64,0},{128,192},{192,128},{256,320},{320,256},{384,448},{4... | collective-permute-start | bytes 454664 | tf_op jit(solution)/shard_map/ppermute | solution.py:20
  24.5 8.3 %collective-permute-start.3 = (f32[144,128]{1,0:T(8,128)S(1)}, f32[144,128]{1,0:T(8,128)S(1)}, u32[]{:S(2)}, u32[]{:S(2)}) collective-permute-start(f32[144,128]{1,0:T(8,128)S(1)} %get-tuple-element.28.own_one), channel_id=1, source_target_pairs={{0,8},{4,12},{8,0},{12,4},{16,24},{20,28},{24,16},{28,20},{32,40},... | collective-permute-start | bytes 221192 | tf_op jit(solution)/shard_map/ppermute | solution.py:20
  30.0 7.3 %collective-permute-start.4 = (f32[336,128]{1,0:T(8,128)S(1)}, f32[336,128]{1,0:T(8,128)S(1)}, u32[]{:S(2)}, u32[]{:S(2)}) collective-permute-start(f32[336,128]{1,0:T(8,128)S(1)} %get-tuple-element.29.own_two), channel_id=1, source_target_pairs={{0,8},{4,12},{8,0},{12,4},{16,24},{20,28},{24,16},{28,20},{32,40},... | collective-permute-start | bytes 516104 | tf_op jit(solution)/shard_map/ppermute | solution.py:20

commit v2 on v1

--- a/solution.py
+++ b/solution.py
@@ -8,7 +8,7 @@
 FACE = 64
 LEAF = 4 * FACE
 MESSAGE = 96 + 3 * 128
-CUT_TWO, CUT_THREE = 184, 144
+CUT_TWO, CUT_THREE = 200, 160
 F32 = jnp.float32
 BF16 = jnp.bfloat16
 

time: 39 us -> 41.7 us (1.069)
  the two profiles are of different devices: /device:TPU:18 before, /device:TPU:1 now
where the time goes in v2:
time: 41.7 us; the launch traced here: 41.5 us
  starting transfers between devices  24.7 us (59%)
  Pallas kernels  12.9 us (31%)
  between operations  2.07 us (5%)
  waiting for transfers between devices  1.76 us (4%)
    ppermute x5, starting transfers between devices, swapped(): lax.ppermute(shard, axis, [(i, i ^ 1 << stride) for i in range(lax.axis_s...  24.7 us
    pallas_call x7, Pallas kernels, run(): pl.pallas_call(kernel, out_shape=out_shape, in_specs=[smem] * scalars + [...  11.9 us
    ppermute x5, waiting for transfers between devices, swapped(): lax.ppermute(shard, axis, [(i, i ^ 1 << stride) for i in range(lax.axis_s...  1.76 us
    pallas_call x1, Pallas kernels, body(): pl.pallas_call(build_kernel, out_shape=jax.ShapeDtypeStruct((LEAF, LEAF),...  1 us
  transfers between devices with their start and end apart: 5, of which 3 were waited for; matrix products, arithmetic and copies ran while one was open for 0% of the time, Pallas kernels for 17%

profile of v2, /device:TPU:1, one launch (start us, length us, event | category | flops | bytes accessed | tf_op | source)
XLA Modules:
  0.0 41.5 jit_solution(12434728132817880711)
XLA Ops:
  1.9 1.0 %leaf_build.1.mine = f32[256,256]{1,0:T(8,128)S(1)} custom-call(s32[1,1]{1,0:T(1,128)S(6)} %copy.8.label, s32[1,1]{1,0:T(1,128)S(6)} %copy.9.flag, f32[1]{0:T(128)S(6)} %copy.7.wave, f32[256,256]{1,0:T(8,128)} %bitcast.5, f32[472,472]{1,0:T(8,128)} %operator.1, f32[8,472]{1,0:T(8,128)} %table_at.1), custom_call_target="tpu_custom_call" | custom-call | tf_op jit(solution)/shard_map/leaf_build/pallas_call | solution.py:479
  2.9 14.2 %collective-permute-start = (f32[256,256]{1,0:T(8,128)S(1)}, f32[256,256]{1,0:T(8,128)S(1)}, u32[]{:S(2)}, u32[]{:S(2)}) collective-permute-start(f32[256,256]{1,0:T(8,128)S(1)} %leaf_build.1.mine), channel_id=1, source_target_pairs={{0,4},{4,0},{8,12},{12,8},{16,20},{20,16},{24,28},{28,24},{32,36},... | collective-permute-start | bytes 786440 | tf_op jit(solution)/shard_map/ppermute | solution.py:20
  17.2 0.1 pad_add_fusion.place
  17.2 1.0 %collective-permute-done.theirs = f32[256,256]{1,0:T(8,128)S(1)} collective-permute-done((f32[256,256]{1,0:T(8,128)S(1)}, f32[256,256]{1,0:T(8,128)S(1)}, u32[]{:S(2)}, u32[]{:S(2)}) %collective-permute-start) | collective-permute-done | bytes 262176 | tf_op jit(solution)/shard_map/ppermute | solution.py:20
  18.3 2.2 %first_merge.1 = (f32[200,128]{1,0:T(8,128)S(1)}, f32[280,128]{1,0:T(8,128)S(1)}, f32[64,128]{1,0:T(8,128)S(1)}, bf16[64,384]{1,0:T(8,128)(2,1)S(1)}, bf16[64,384]{1,0:T(8,128)(2,1)S(1)}) custom-call(s32[3]{0:T(128)S(1)} %pad_add_fusion.place, f32[256,256]{1,0:T(8,128)S(1)} %leaf_build.1.mine, f32[256,256]{1,0:T(8,128)S(1)} %collective-permute-done.theirs), custom_call_target="tpu_custom_call" | custom-call | tf_op jit(solution)/shard_map/first_merge/pallas_call | solution.py:464
  20.5 1.9 %collective-permute-start.1 = (f32[200,128]{1,0:T(8,128)S(1)}, f32[200,128]{1,0:T(8,128)S(1)}, u32[]{:S(2)}, u32[]{:S(2)}) collective-permute-start(f32[200,128]{1,0:T(8,128)S(1)} %get-tuple-element.21.own.own_one), channel_id=1, source_target_pairs={{0,64},{64,0},{128,192},{192,128},{256,320},{320,256},{384,448},{4... | collective-permute-start | bytes 307208 | tf_op jit(solution)/shard_map/ppermute | solution.py:20
  22.4 3.4 %collective-permute-start.2 = (f32[280,128]{1,0:T(8,128)S(1)}, f32[280,128]{1,0:T(8,128)S(1)}, u32[]{:S(2)}, u32[]{:S(2)}) collective-permute-start(f32[280,128]{1,0:T(8,128)S(1)} %get-tuple-element.22.own_two), channel_id=1, source_target_pairs={{0,64},{64,0},{128,192},{192,128},{256,320},{320,256},{384,448},{4... | collective-permute-start | bytes 430088 | tf_op jit(solution)/shard_map/ppermute | solution.py:20
  25.8 0.9 %first_rows.1.outer = f32[96,384]{1,0:T(8,128)S(1)} custom-call(s32[3]{0:T(128)S(1)} %pad_add_fusion.place, f32[256,256]{1,0:T(8,128)S(1)} %leaf_build.1.mine, f32[256,256]{1,0:T(8,128)S(1)} %collective-permute-done.theirs, bf16[64,384]{1,0:T(8,128)(2,1)S(1)} %get-tuple-element.24.solved_high, bf16[64,384]{1,0:T(8,128)(2,1)S(1)} %get-tuple-element.25.solved_low), custom_call_target="tpu_custom_call" | custom-call | tf_op jit(solution)/shard_map/first_rows/pallas_call | solution.py:464
  26.6 0.0 collective-permute-done.1.received.received_one
  26.6 2.6 %second_inverse.1 = (bf16[128,128]{1,0:T(8,128)(2,1)S(1)}, bf16[128,128]{1,0:T(8,128)(2,1)S(1)}, bf16[96,128]{1,0:T(8,128)(2,1)S(1)}, bf16[96,128]{1,0:T(8,128)(2,1)S(1)}) custom-call(f32[200,128]{1,0:T(8,128)S(1)} %get-tuple-element.21.own.own_one, f32[200,128]{1,0:T(8,128)S(1)} %collective-permute-done.1.received.received_one, f32[96,384]{1,0:T(8,128)S(1)} %first_rows.1.outer), custom_call_target="tpu_custom_call" | custom-call | flops 10000000000 | bytes 100000000 | tf_op jit(solution)/shard_map/second_inverse/pallas_call | solution.py:464
  29.3 0.5 %collective-permute-done.2.received_two = f32[280,128]{1,0:T(8,128)S(1)} collective-permute-done((f32[280,128]{1,0:T(8,128)S(1)}, f32[280,128]{1,0:T(8,128)S(1)}, u32[]{:S(2)}, u32[]{:S(2)}) %collective-permute-start.2) | collective-permute-done | bytes 143392 | tf_op jit(solution)/shard_map/ppermute | solution.py:20
  29.8 1.0 %second_merge.1 = (f32[160,128]{1,0:T(8,128)S(1)}, f32[320,128]{1,0:T(8,128)S(1)}, bf16[128,512]{1,0:T(8,128)(2,1)S(1)}, bf16[128,512]{1,0:T(8,128)(2,1)S(1)}) custom-call(s32[3]{0:T(128)S(1)} %pad_add_fusion.place, f32[200,128]{1,0:T(8,128)S(1)} %get-tuple-element.21.own.own_one, f32[280,128]{1,0:T(8,128)S(1)} %get-tuple-element.22.own_two, ...), custom_call_target="tpu_custom_call" | custom-call | tf_op jit(solution)/shard_map/second_merge/pallas_call | solution.py:464
  30.8 1.9 %collective-permute-start.3 = (f32[160,128]{1,0:T(8,128)S(1)}, f32[160,128]{1,0:T(8,128)S(1)}, u32[]{:S(2)}, u32[]{:S(2)}) collective-permute-start(f32[160,128]{1,0:T(8,128)S(1)} %get-tuple-element.28.own_one), channel_id=1, source_target_pairs={{0,8},{4,12},{8,0},{12,4},{16,24},{20,28},{24,16},{28,20},{32,40},... | collective-permute-start | bytes 245768 | tf_op jit(solution)/shard_map/ppermute | solution.py:20
  32.7 3.4 %collective-permute-start.4 = (f32[320,128]{1,0:T(8,128)S(1)}, f32[320,128]{1,0:T(8,128)S(1)}, u32[]{:S(2)}, u32[]{:S(2)}) collective-permute-start(f32[320,128]{1,0:T(8,128)S(1)} %get-tuple-element.29.own_two), channel_id=1, source_target_pairs={{0,8},{4,12},{8,0},{12,4},{16,24},{20,28},{24,16},{28,20},{32,40},... | collective-permute-start | bytes 491528 | tf_op jit(solution)/shard_map/ppermute | solution.py:20
  36.1 0.9 %second_rows.1.rows = f32[96,512]{1,0:T(8,128)S(1)} custom-call(s32[3]{0:T(128)S(1)} %pad_add_fusion.place, f32[96,384]{1,0:T(8,128)S(1)} %first_rows.1.outer, bf16[96,128]{1,0:T(8,128)(2,1)S(1)} %get-tuple-element.30.outer_high, bf16[96,128]{1,0:T(8,128)(2,1)S(1)} %get-tuple-element.31.outer_low, bf16[128,128]{1,0:T(8,128)(2,1)S(1)} %get-tuple-element.26.inverse_high, ...), custom_call_target="tpu_custom_call" | custom-call | tf_op jit(solution)/shard_map/second_rows/pallas_call | solution.py:464
  37.0 0.0 collective-permute-done.3.received.received_one
  37.0 2.9 %third_inverse.1 = (f32[96,384]{1,0:T(8,128)S(1)}, bf16[96,128]{1,0:T(8,128)(2,1)S(1)}, bf16[96,128]{1,0:T(8,128)(2,1)S(1)}) custom-call(f32[160,128]{1,0:T(8,128)S(1)} %get-tuple-element.28.own_one, f32[320,128]{1,0:T(8,128)S(1)} %get-tuple-element.29.own_two, f32[160,128]{1,0:T(8,128)S(1)} %collective-permute-done.3.received.received_one, ...), custom_call_target="tpu_custom_call" | custom-call | flops 10000000000 | bytes 100000000 | tf_op jit(solution)/shard_map/third_inverse/pallas_call | solution.py:464
  39.8 0.2 collective-permute-done.4.received_two
  40.1 1.4 %third_merge.1 = f32[96,768]{1,0:T(8,128)} custom-call(s32[3]{0:T(128)S(1)} %pad_add_fusion.place, f32[96,384]{1,0:T(8,128)S(1)} %get-tuple-element.34.half, f32[160,128]{1,0:T(8,128)S(1)} %collective-permute-done.3.received.received_one, f32[320,128]{1,0:T(8,128)S(1)} %collective-permute-done.4.received_two, ...), custom_call_target="tpu_custom_call" | custom-call | tf_op jit(solution)/shard_map/third_merge/pallas_call | solution.py:464
Async XLA Ops:
  2.9 15.3 %collective-permute-start = (f32[256,256]{1,0:T(8,128)S(1)}, f32[256,256]{1,0:T(8,128)S(1)}, u32[]{:S(2)}, u32[]{:S(2)}) collective-permute-start(f32[256,256]{1,0:T(8,128)S(1)} %leaf_build.1.mine), channel_id=1, source_target_pairs={{0,4},{4,0},{8,12},{12,8},{16,20},{20,16},{24,28},{28,24},{32,36},... | collective-permute-start | bytes 786440 | tf_op jit(solution)/shard_map/ppermute | solution.py:20
  20.5 6.2 %collective-permute-start.1 = (f32[200,128]{1,0:T(8,128)S(1)}, f32[200,128]{1,0:T(8,128)S(1)}, u32[]{:S(2)}, u32[]{:S(2)}) collective-permute-start(f32[200,128]{1,0:T(8,128)S(1)} %get-tuple-element.21.own.own_one), channel_id=1, source_target_pairs={{0,64},{64,0},{128,192},{192,128},{256,320},{320,256},{384,448},{4... | collective-permute-start | bytes 307208 | tf_op jit(solution)/shard_map/ppermute | solution.py:20
  22.4 7.4 %collective-permute-start.2 = (f32[280,128]{1,0:T(8,128)S(1)}, f32[280,128]{1,0:T(8,128)S(1)}, u32[]{:S(2)}, u32[]{:S(2)}) collective-permute-start(f32[280,128]{1,0:T(8,128)S(1)} %get-tuple-element.22.own_two), channel_id=1, source_target_pairs={{0,64},{64,0},{128,192},{192,128},{256,320},{320,256},{384,448},{4... | collective-permute-start | bytes 430088 | tf_op jit(solution)/shard_map/ppermute | solution.py:20
  30.8 6.2 %collective-permute-start.3 = (f32[160,128]{1,0:T(8,128)S(1)}, f32[160,128]{1,0:T(8,128)S(1)}, u32[]{:S(2)}, u32[]{:S(2)}) collective-permute-start(f32[160,128]{1,0:T(8,128)S(1)} %get-tuple-element.28.own_one), channel_id=1, source_target_pairs={{0,8},{4,12},{8,0},{12,4},{16,24},{20,28},{24,16},{28,20},{32,40},... | collective-permute-start | bytes 245768 | tf_op jit(solution)/shard_map/ppermute | solution.py:20
  32.7 7.4 %collective-permute-start.4 = (f32[320,128]{1,0:T(8,128)S(1)}, f32[320,128]{1,0:T(8,128)S(1)}, u32[]{:S(2)}, u32[]{:S(2)}) collective-permute-start(f32[320,128]{1,0:T(8,128)S(1)} %get-tuple-element.29.own_two), channel_id=1, source_target_pairs={{0,8},{4,12},{8,0},{12,4},{16,24},{20,28},{24,16},{28,20},{32,40},... | collective-permute-start | bytes 491528 | tf_op jit(solution)/shard_map/ppermute | solution.py:20
